TPU v7x, 512 devices: a whole 4x4x16 slice. The times are simulated.
512 devices in a mesh: dp: 32 (over y, z_hi, x), tensor: 16 (over z_lo, core).
Axes of the slice: x: 4, y: 4, z: 16 (z_hi: 2, z_lo: 8; z = z_hi * 8 + z_lo), core: 2. Of those that a mesh axis runs over, the one named last changes fastest.
Arguments:
- context: bfloat16 [2048, 8192], P('tensor', 'dp'), may hold values from -6 to 6
- out_weight: bfloat16 [8192, 8192], P('dp', 'tensor'), may hold values from -0.125 to 0.125
- residual: bfloat16 [2048, 8192], P('dp', 'tensor'), may hold values from -6 to 6
- final_states: bfloat16 [2048, 8192], P('dp', 'tensor'), may hold values from -6 to 6
Outputs:
- gram: float32 [8192, 8192], P('dp', 'tensor')
- cross: float32 [8192, 8192], P('dp', 'tensor')
All inputs are finite; a program needn't handle non-finite values.
Results may differ from a plain program's by a relative error of at most 0.0035.
Values may be sent and summed in bfloat16 or wider, within the bound.
A program may use at most 64 MiB of HBM per device.

v0:
```python
import jax
import jax.numpy as jnp
from jax import lax
from jax.sharding import PartitionSpec as P


def broadcast(value, axis, source):
    kept = jnp.where(lax.axis_index(axis) == source, value, 0).astype(value.dtype)
    return lax.psum(kept, axis)


def body(context, out_weight, residual, final_states):
    ratio = lax.axis_size("dp") // lax.axis_size("tensor")
    place = lax.axis_index("dp")
    sub_width = out_weight.shape[0]
    tok_dev = residual.shape[0]
    partial_out = jnp.dot(
        lax.all_gather(context, "tensor", axis=0, tiled=True),
        out_weight,
        preferred_element_type=jnp.float32,
    )
    total = partial_out.shape[0]
    anchor = place * tok_dev
    own_rows = lax.dynamic_slice_in_dim(partial_out, anchor, tok_dev, 0) + residual.astype(
        jnp.float32
    )
    partial_out = lax.dynamic_update_slice_in_dim(partial_out, own_rows, anchor, 0)
    summed = lax.psum(partial_out, "dp")
    states = summed.astype(jnp.bfloat16)
    final_all = lax.all_gather(final_states, "dp", axis=0, tiled=True)
    half_index = place % ratio
    root_index = place // ratio
    own_half = lax.dynamic_slice_in_dim(states, half_index * sub_width, sub_width, 1)
    left_block = broadcast(own_half, "tensor", root_index)
    contract = (((0,), (0,)), ((), ()))
    gram = lax.dot_general(left_block, states, contract, preferred_element_type=jnp.float32) / total
    cross = (
        lax.dot_general(left_block, final_all, contract, preferred_element_type=jnp.float32) / total
    )
    return (gram, cross)


def solution(mesh):
    in_specs = (P("tensor", "dp"), P("dp", "tensor"), P("dp", "tensor"), P("dp", "tensor"))
    out_specs = (P("dp", "tensor"), P("dp", "tensor"))
    return jax.shard_map(body, mesh=mesh, in_specs=in_specs, out_specs=out_specs, check_vma=False)
```

profile of v0, /device:TPU:25, one launch (start us, length us, event | category | flops | bytes accessed | tf_op | source)
XLA Modules:
  0.0 801.9 jit_solution(6133093497754974444)
XLA Ops:
  8.0 0.0 copy-start
  8.0 0.0 all-gather.3.cloned.1.call-start
  8.1 0.7 all-gather.3.cloned.1.call-update
  8.7 0.0 all-reduce.3.cloned.1.call-start
  8.8 0.0 copy-start.1
  8.8 104.9 %all-gather.3.cloned.1.call-done = bf16[2048,256]{1,0:T(8,128)(2,1)} async-done(((bf16[128,256]{1,0:T(8,128)(2,1)}), bf16[2048,256]{1,0:T(8,128)(2,1)}) %all-gather.3.cloned.1.call-update) | async-done | bytes 1048592 | tf_op jit(solution)/shard_map/all_gather | solution.py:18
  113.7 0.0 copy-done
  113.7 3.9 fusion
  117.6 0.0 copy-done.1
  117.6 1.6 add_dynamic-update-slice_fusion
  119.1 422.6 %all-reduce.4 = bf16[2048,512]{1,0:T(8,128)(2,1)S(1)} all-reduce(f32[2048,512]{1,0:T(8,128)} %add_dynamic-update-slice_fusion), channel_id=1, replica_groups=mesh['dp'=32,'tensor'=16] {'dp'}, use_global_device_ids=true, to_apply=%region_0.0 | all-reduce | flops 1048576 | bytes 6291456 | tf_op jit(solution)/shard_map/psum | solution.py:28
  541.8 1.2 dynamic-slice_select_fusion
  543.0 0.0 all-reduce.3.cloned.1.call-update
  543.0 0.0 all-gather.5.cloned.1.call-start
  543.0 0.5 all-gather.5.cloned.1.call-update
  543.6 244.9 %all-reduce.3.cloned.1.call-done = bf16[2048,256]{1,0:T(8,128)(2,1)} async-done(((bf16[2048,256]{1,0:T(8,128)(2,1)}), bf16[2048,256]{1,0:T(8,128)(2,1)}) %all-reduce.3.cloned.1.call-update) | async-done | bytes 1048592 | tf_op jit(solution)/shard_map/psum | solution.py:9
  788.5 0.0 copy-start.2
  788.5 2.8 convolution_multiply_fusion.1
  791.3 0.0 all-gather.5.cloned.1.call-done
  791.3 0.0 copy-done.2
  791.3 3.1 convolution_multiply_fusion
Async XLA Ops:
  8.0 105.7 %copy-start = (bf16[256,512]{1,0:T(8,128)(2,1)S(1)}, bf16[256,512]{1,0:T(8,128)(2,1)}, u32[]{:S(2)}) copy-start(bf16[256,512]{1,0:T(8,128)(2,1)} %param.5) | copy-start | bytes 786436
  8.0 105.7 %all-gather.3.cloned.1.call-start = ((), (), s32[]{:S(2)}) async-start(), calls=%async_computation | async-start | bytes 1114112 | tf_op jit(solution)/shard_map/all_gather | solution.py:18
  8.7 779.7 %all-reduce.3.cloned.1.call-start = ((), (), s32[]{:S(2)}) async-start(), calls=%async_computation.1 | async-start | bytes 2097152 | tf_op jit(solution)/shard_map/psum | solution.py:9
  8.8 108.8 %copy-start.1 = (bf16[64,512]{1,0:T(8,128)(2,1)S(1)}, bf16[64,512]{1,0:T(8,128)(2,1)}, u32[]{:S(2)}) copy-start(bf16[64,512]{1,0:T(8,128)(2,1)} %param.6) | copy-start | bytes 196612
  543.0 248.3 %all-gather.5.cloned.1.call-start = ((), (), s32[]{:S(2)}) async-start(), calls=%async_computation.2 | async-start | bytes 2162688 | tf_op jit(solution)/shard_map/all_gather | solution.py:30
  788.5 2.8 copy-start.2
Sparse Core Ops, SparseCore 0:
  10.9 102.7 all-gather.2
  543.1 245.3 all-reduce.2
Sparse Core Ops, SparseCore 1:
  548.7 144.5 all-gather.4
where the time goes:
time: 803 us; the launch traced here: 802 us
  blocking collectives  423 us (53%)
  waiting for transfers between devices  351 us (44%)
  between operations  15.5 us (2%)
  matrix products  9.81 us (1%)
    psum x1, blocking collectives, body(): summed = lax.psum(partial_out, 'dp')  423 us
    psum x1, waiting for transfers between devices, broadcast(): return lax.psum(kept, axis)  245 us
    all_gather x1, waiting for transfers between devices, body(): lax.all_gather(context, 'tensor', axis=0, tiled=True)  105 us
  transfers between devices with their start and end apart: 3, of which 2 were waited for; matrix products, arithmetic and copies ran while one was open for 0% of the time, Pallas kernels for 0%

commit v1 on v0

v1 whole, which is shorter than its diff:
```python
import jax
import jax.numpy as jnp
from jax import lax
from jax.experimental import pallas as pl
from jax.experimental.pallas import tpu as pltpu
from jax.sharding import PartitionSpec as P

MESH = pl.DeviceIdType.MESH
OFFSETS = (0, -1, 1, -2)
LEVELS = (
    ((1, 0), (2, 0), (0, 1), (0, 2)),
    ((3, 0), (1, 1), (2, 1), (1, 2), (2, 2), (0, 3)),
    ((3, 1), (3, 2), (1, 3), (2, 3)),
    ((3, 3),),
)
ORDER = ((0, 0), (1, 0), (0, 1), (2, 0), (0, 2), (1, 1), (1, 2), (2, 1), (2, 2), (3, 0), (0, 3), (1, 3), (3, 1), (2, 3), (3, 2), (3, 3))


class Place:
    def __init__(self):
        d, t = lax.axis_index("dp"), lax.axis_index("tensor")
        self.y, self.zh, self.x = d // 8, (d // 4) % 2, d % 4
        self.zl, self.c = t // 2, t % 2
        self.q = self.y * 4 + self.x
        self.sg = 1 - 2 * self.c

    def at(self, y=None, zh=None, x=None, zl=None, c=None):
        y, zh, x, zl, c = (b if a is None else a for a, b in zip((y, zh, x, zl, c), (self.y, self.zh, self.x, self.zl, self.c)))
        return y * 8 + zh * 4 + x, zl * 2 + c


class Sends:
    def __init__(self):
        self.pending = []

    def start(self, src, dst, send_sem, recv_sem, device, cond=None):
        copy = pltpu.make_async_remote_copy(
            src_ref=src, dst_ref=dst, send_sem=send_sem, recv_sem=recv_sem, device_id=device, device_id_type=MESH
        )
        if cond is None:
            copy.start()
        else:
            pl.when(cond)(copy.start)
        self.pending.append((copy, cond))

    def drain(self):
        for copy, cond in self.pending:
            if cond is None:
                copy.wait_send()
            else:
                pl.when(cond)(copy.wait_send)
        self.pending = []


def arrived(ref, sem, device):
    pltpu.make_async_remote_copy(
        src_ref=ref, dst_ref=ref, send_sem=sem, recv_sem=sem, device_id=device, device_id_type=MESH
    ).wait_recv()


class Gather:
    def __init__(self, me, sends, own, slot, ssem, rsem):
        self.me, self.sends, self.own, self.slot, self.ssem, self.rsem = me, sends, own, slot, ssem, rsem

    def source(self, h, i, j):
        a, b = (i, j) if h == 0 else (j, i)
        return (self.me.x + self.me.sg * OFFSETS[a] + 8) % 4, (self.me.y + self.me.sg * OFFSETS[b] + 8) % 4

    def send(self, h, have, give, axis, sign):
        me = self.me
        px, py = self.source(h, *have)
        dst = self.slot(h, px, py)
        src = self.own(h) if have == (0, 0) else dst
        along_x = (axis == 0) == (h == 0)
        if along_x:
            device = me.at(x=(me.x + sign * me.sg + 4) % 4)
        else:
            device = me.at(y=(me.y + sign * me.sg + 4) % 4)
        k = h * 16 + give[0] * 4 + give[1]
        self.sends.start(src, dst, self.ssem.at[k], self.rsem.at[k], device)

    def begin(self, h):
        self.send(h, (0, 0), (1, 0), 0, 1)
        self.send(h, (0, 0), (2, 0), 0, -1)
        self.send(h, (0, 0), (0, 1), 1, 1)
        self.send(h, (0, 0), (0, 2), 1, -1)

    def event(self, h, i, j):
        px, py = self.source(h, i, j)
        arrived(self.slot(h, px, py), self.rsem.at[h * 16 + i * 4 + j], self.me.at(c=1 - self.me.c))
        if j == 0:
            if i == 1:
                self.send(h, (1, 0), (3, 0), 0, 1)
            self.send(h, (i, 0), (i, 1), 1, 1)
            self.send(h, (i, 0), (i, 2), 1, -1)
        elif j == 1:
            self.send(h, (i, 1), (i, 3), 1, 1)

    def level(self, n):
        for i, j in LEVELS[n]:
            for h in (0, 1):
                self.event(h, i, j)


def kernel(
    ctx, w, res, fin, gram, cross,
    wbuf, cbuf, rbuf, part, other, fbuf, sbuf, lbuf,
    w_s, w_r, f_s, f_r, s_s, s_r, a_s, a_r, z_s, z_r, b_s, b_r, e_s, e_r, x_s, x_r, l_s, l_r, own_sem,
):
    me = Place()
    sends = Sends()
    sibling = me.at(c=1 - me.c)
    partner = me.at(zh=1 - me.zh)

    barrier = pltpu.get_barrier_semaphore()

    def greet(device):
        pl.semaphore_signal(barrier, inc=1, device_id=device, device_id_type=MESH)

    for k in range(1, 16):
        p = (me.q + k) % 16
        greet(me.at(y=p // 4, x=p % 4))
    for k in range(16):
        greet(me.at(y=k // 4, x=k % 4, c=1 - me.c))
    for k in range(1, 8):
        greet(me.at(zl=(me.zl + k) % 8))
    greet(partner)
    pl.semaphore_wait(barrier, 15 + 16 + 7 + 1)

    slot_of = lambda zl: (zl % 2) * 4 + zl // 2
    lanes = pl.ds(pl.multiple_of(me.q * 256, 256), 256)
    for i in range(8):
        p = 8 * me.c + i
        src, dst = ctx.at[pl.ds(16 * i, 16)], cbuf.at[slot_of(me.zl), :, lanes]
        k = me.q % 8
        mine = (p == me.q) & (me.q // 8 == me.c)
        sends.start(src, dst, a_s.at[i], a_r.at[k], me.at(y=p // 4, x=p % 4, c=me.q // 8), cond=jnp.logical_not(mine))
        pl.when(mine)(pltpu.make_async_copy(src, dst, a_r.at[k]).start)

    gather_w = Gather(
        me, sends,
        lambda h: w.at[pl.ds(128 * h, 128)],
        lambda h, px, py: wbuf.at[py * 4 + px, pl.ds(128 * h, 128)],
        w_s, w_r,
    )
    gather_w.begin(0)
    gather_w.begin(1)
    own_w = pltpu.make_async_copy(w, wbuf.at[me.q], own_sem.at[0])
    own_w.start()

    own_f = pltpu.make_async_copy(fin, fbuf.at[me.zh, me.y, pl.ds(4 * me.x, 4)], own_sem.at[1])
    own_f.start()
    sends.start(fin, fbuf.at[me.zh, me.y, pl.ds(4 * me.x, 4)], x_s.at[0], x_r.at[0], partner)

    for j in range(4):
        mine = (me.x == me.y) & (me.x == j)
        sends.start(res.at[j], rbuf.at[me.y], e_s.at[j], e_r.at[me.y], me.at(y=me.x, x=j), cond=jnp.logical_not(mine))
        pl.when(mine)(pltpu.make_async_copy(res.at[j], rbuf.at[me.y], e_r.at[me.y]).start)

    half = pl.ds(pl.multiple_of(me.c * 2048, 2048), 2048)
    other_half = pl.ds(pl.multiple_of((1 - me.c) * 2048, 2048), 2048)
    for i in range(8):
        piece = cbuf.at[slot_of(me.zl), :, pl.ds(pl.multiple_of((me.c * 8 + i) * 256, 256), 256)]
        arrived(piece, a_r.at[i], sibling)
    piece = cbuf.at[slot_of(me.zl), :, half]
    for k in range(1, 8):
        sends.start(piece, piece, z_s.at[k], z_r.at[k], me.at(zl=(me.zl + k) % 8))
    sends.start(piece, piece, b_s.at[0], b_r.at[0], sibling)

    def along_z(k):
        piece = cbuf.at[slot_of((me.zl - k + 8) % 8), :, half]
        arrived(piece, z_r.at[k], sibling)
        sends.start(piece, piece, b_s.at[k], b_r.at[k], sibling)

    gather_w.level(0)
    along_z(1)
    along_z(7)
    gather_w.level(1)
    for k in (2, 6, 3, 5, 4):
        along_z(k)
    gather_w.level(2)
    gather_w.level(3)
    for k in range(8):
        arrived(cbuf.at[slot_of((me.zl - k + 8) % 8), :, other_half], b_r.at[k], sibling)
    own_w.wait()

    part[...] = jnp.zeros_like(part)

    def project(k, carry):
        cols = pl.ds(pl.multiple_of(k * 512, 512), 512)
        a = cbuf[:, :, cols].reshape(128, 512)
        b = wbuf[pl.ds(2 * k, 2)].reshape(512, 512)
        part[...] += jnp.dot(a, b, preferred_element_type=jnp.float32).reshape(8, 16, 512)
        return carry

    lax.fori_loop(0, 8, project, 0)
    for j in range(4):
        arrived(rbuf.at[j], e_r.at[j], sibling)
    mine = pl.ds(4 * me.zh, 4)
    part[mine] = part[mine] + rbuf[...].astype(jnp.float32)
    sends.start(part, other, x_s.at[1], x_r.at[1], partner)

    own_f.wait()
    fslot = lambda h, px, py: fbuf.at[h, py, pl.ds(4 * px, 4)]
    arrived(fbuf.at[1 - me.zh, me.y, pl.ds(4 * me.x, 4)], x_r.at[0], sibling)
    gather_f = Gather(me, sends, lambda h: fslot(h, me.x, me.y), fslot, f_s, f_r)
    gather_f.begin(0)
    gather_f.begin(1)
    for n in range(4):
        gather_f.level(n)

    arrived(other, x_r.at[1], sibling)
    sbuf[:, me.q] = (part[...] + other[...]).astype(jnp.bfloat16)
    sslot = lambda h, px, py: sbuf.at[pl.ds(4 * h, 4), py * 4 + px]
    gather_s = Gather(me, sends, lambda h: sslot(h, me.x, me.y), sslot, s_s, s_r)
    gather_s.begin(0)
    gather_s.begin(1)

    lead = me.x // 2
    on_line = me.c == lead
    root = 2 * me.y + me.zh
    is_root = on_line & (me.zl == root)
    fed = on_line & (me.zl != root)
    lsg = 1 - 2 * lead
    lcols = pl.ds(pl.multiple_of((me.x % 2) * 256, 256), 256)
    above, below = me.zl > root, me.zl < root
    up_hop, down_hop = (8 - root) // 2, (root + 1) // 2
    o_up, o_down = me.zl - root, root - me.zl
    has_up = on_line & (
        ((me.zl == root) & (root < 7))
        | (above & (o_up >= up_hop) & (me.zl < 7))
        | (below & (o_down <= down_hop) & (o_down > 1))
    )
    has_down = on_line & (
        ((me.zl == root) & (root > 0))
        | (below & (o_down >= down_hop) & (me.zl > 0))
        | (above & (o_up <= up_hop) & (o_up > 1))
    )
    at_root = jnp.where(me.zl == root, 1, 0)
    up_zl = jnp.minimum(me.zl + at_root * up_hop + (1 - at_root), 7)
    down_zl = jnp.maximum(me.zl - at_root * down_hop - (1 - at_root), 0)

    def place_of(m):
        a, b = ORDER[m]
        px, py = (me.x + lsg * OFFSETS[a] + 8) % 4, (me.y + lsg * OFFSETS[b] + 8) % 4
        return py * 4 + px

    def pass_on(m, who):
        piece = lbuf.at[:, place_of(m)]
        sends.start(piece, piece, l_s.at[m], l_r.at[m], me.at(zl=up_zl), cond=has_up & who)
        sends.start(piece, piece, l_s.at[16 + m], l_r.at[m], me.at(zl=down_zl), cond=has_down & who)
        sends.start(piece, piece, l_s.at[32 + m], l_r.at[16 + m], sibling, cond=who)

    def root_sends(m):
        place = place_of(m)

        @pl.when(is_root)
        def _():
            lbuf[:, place] = sbuf[:, place, :, lcols]

        pass_on(m, is_root)

    def take(m):
        piece = lbuf.at[:, place_of(m)]
        pl.when(fed)(lambda: arrived(piece, l_r.at[m], sibling))
        pass_on(m, fed)
        pl.when(jnp.logical_not(on_line))(lambda: arrived(piece, l_r.at[16 + m], sibling))

    root_sends(0)
    gather_s.level(0)
    for m in range(1, 5):
        root_sends(m)
    gather_s.level(1)
    for m in range(5, 11):
        root_sends(m)
    gather_s.level(2)
    for m in range(11, 15):
        root_sends(m)
    for m in range(8):
        take(m)
    gather_s.level(3)
    root_sends(15)

    gram[...] = jnp.zeros_like(gram)
    cross[...] = jnp.zeros_like(cross)

    def add(m):
        place = place_of(m)
        a = lbuf[:, place].reshape(128, 256)
        s = sbuf[:, place].reshape(128, 512)
        f = fbuf[:, :, place].reshape(128, 512)
        dims = (((0,), (0,)), ((), ()))
        gram[...] += lax.dot_general(a, s, dims, preferred_element_type=jnp.float32)
        cross[...] += lax.dot_general(a, f, dims, preferred_element_type=jnp.float32)

    for m in range(8, 16):
        take(m)
        add(2 * (m - 8))
        add(2 * (m - 8) + 1)
    gram[...] = gram[...] * (1.0 / 2048)
    cross[...] = cross[...] * (1.0 / 2048)
    sends.drain()


def body(context, out_weight, residual, final_states):
    vmem = pl.BlockSpec(memory_space=pltpu.VMEM)
    dma = lambda n: pltpu.SemaphoreType.DMA((n,))
    bf16, f32 = jnp.bfloat16, jnp.float32
    out = jax.ShapeDtypeStruct((256, 512), f32)
    return pl.pallas_call(
        kernel,
        out_shape=(out, out),
        in_specs=[vmem] * 4,
        out_specs=(vmem, vmem),
        scratch_shapes=[
            pltpu.VMEM((16, 256, 512), bf16),
            pltpu.VMEM((8, 16, 4096), bf16),
            pltpu.VMEM((4, 16, 512), bf16),
            pltpu.VMEM((8, 16, 512), f32),
            pltpu.VMEM((8, 16, 512), f32),
            pltpu.VMEM((2, 4, 16, 16, 512), bf16),
            pltpu.VMEM((8, 16, 16, 512), bf16),
            pltpu.VMEM((8, 16, 16, 256), bf16),
            dma(32), dma(32), dma(32), dma(32), dma(32), dma(32),
            dma(8), dma(8), dma(8), dma(8), dma(8), dma(8),
            dma(4), dma(4), dma(2), dma(2), dma(48), dma(32), dma(2),
        ],
        compiler_params=pltpu.CompilerParams(collective_id=0, has_side_effects=True, vmem_limit_bytes=40 << 20),
        cost_estimate=pl.CostEstimate(flops=1 << 31, bytes_accessed=1 << 21, transcendentals=0),
    )(context, out_weight, residual.reshape(4, 16, 512), final_states.reshape(4, 16, 512))


def solution(mesh):
    in_specs = (P("tensor", "dp"), P("dp", "tensor"), P("dp", "tensor"), P("dp", "tensor"))
    out_specs = (P("dp", "tensor"), P("dp", "tensor"))
    return jax.shard_map(body, mesh=mesh, in_specs=in_specs, out_specs=out_specs, check_vma=False)
```

time: 803 us -> 127 us (0.16)
  blocking collectives: 423 us -> 0 us
  waiting for transfers between devices: 351 us -> 0 us
  Pallas kernels: 0 us -> 121 us
  between operations: 15.5 us -> 0.65 us
  matrix products: 9.81 us -> 0 us
    psum x1 -> x0, blocking collectives: 423 us -> none  [body(): summed = lax.psum(partial_out, 'dp')]
    psum x1 -> x0, waiting for transfers between devices: 245 us -> none  [broadcast(): return lax.psum(kept, axis)]
    pallas_call x0 -> x1, Pallas kernels: none -> 121 us  [body(): pl.pallas_call(kernel, out_shape=(out, out), in_specs=[vmem] * 4, out_spe...]
    all_gather x2 -> x0, waiting for transfers between devices: 105 us -> none  [the longest x1 105 us: body(): lax.all_gather(context, 'tensor', axis=0, tiled=True)]
    dot_general x3 -> x0, matrix products: 9.81 us -> none  [the longest x1 3.87 us: body(): jnp.dot(lax.all_gather(context, 'tensor', axis=0, tiled=True), out_weight...]
  transfers between devices with their start and end apart: 3 -> 0, of which waited for: 2 -> 0; matrix products, arithmetic and copies ran while one was open for 0% -> 0% of each run, Pallas kernels for 0% -> 0%
where the time goes in v1:
time: 127 us; the launch traced here: 126 us
  Pallas kernels  121 us (95%)
  local copies, waits for them, and re-layouts  5.05 us (4%)
    pallas_call x1, Pallas kernels, body(): pl.pallas_call(kernel, out_shape=(out, out), in_specs=[vmem] * 4, out_spe...  121 us
    unnamed x10, local copies, waits for them, and re-layouts  5.05 us

profile of v1, /device:TPU:25, one launch (start us, length us, event | category | flops | bytes accessed | tf_op | source)
XLA Modules:
  0.0 126.4 jit_solution(13579087076658806100)
XLA Ops:
  0.6 0.0 copy-start
  0.6 0.9 copy-done
  1.6 0.0 copy-start.1
  1.6 0.8 copy-done.1
  2.4 0.0 copy-start.2
  2.4 0.8 copy-done.2
  3.3 0.0 copy-start.3
  3.3 0.8 copy-done.3
  4.1 120.7 %shard_map.59 = (f32[256,512]{1,0:T(8,128)S(1)}, f32[256,512]{1,0:T(8,128)S(1)}) custom-call(bf16[128,256]{1,0:T(8,128)(2,1)S(1)} %copy-done.1, bf16[256,512]{1,0:T(8,128)(2,1)S(1)} %copy-done, bf16[4,16,512]{2,1,0:T(8,128)(2,1)S(1)} %bitcast.2, bf16[4,16,512]{2,1,0:T(8,128)(2,1)S(1)} %bitcast.3), custom_call_target="tpu_custom_call" | custom-call | flops 2147483648 | bytes 2097152 | tf_op jit(solution)/shard_map/pallas_call | solution.py:310
  124.9 0.8 copy.8
  125.6 0.8 copy.9
Async XLA Ops:
  0.6 1.0 copy-start
  1.6 0.8 copy-start.1
  2.4 0.8 copy-start.2
  3.3 0.8 copy-start.3

commit v2 on v1

v2 whole, which is shorter than its diff:
```python
import jax
import jax.numpy as jnp
from jax import lax
from jax.experimental import pallas as pl
from jax.experimental.pallas import tpu as pltpu
from jax.sharding import PartitionSpec as P

MESH = pl.DeviceIdType.MESH
OFFSETS = (0, -1, 1, -2)
LEVELS = (
    ((1, 0), (2, 0), (0, 1), (0, 2)),
    ((3, 0), (1, 1), (2, 1), (1, 2), (2, 2), (0, 3)),
    ((3, 1), (3, 2), (1, 3), (2, 3)),
    ((3, 3),),
)
class Place:
    def __init__(self):
        d, t = lax.axis_index("dp"), lax.axis_index("tensor")
        self.y, self.zh, self.x = d // 8, (d // 4) % 2, d % 4
        self.zl, self.c = t // 2, t % 2
        self.q = self.y * 4 + self.x
        self.n = self.x * 4 + self.y
        self.sg = 1 - 2 * self.c

    def at(self, y=None, zh=None, x=None, zl=None, c=None):
        y, zh, x, zl, c = (b if a is None else a for a, b in zip((y, zh, x, zl, c), (self.y, self.zh, self.x, self.zl, self.c)))
        return y * 8 + zh * 4 + x, zl * 2 + c


class Sends:
    def __init__(self):
        self.pending = []

    def start(self, src, dst, send_sem, recv_sem, device, cond=None):
        copy = pltpu.make_async_remote_copy(
            src_ref=src, dst_ref=dst, send_sem=send_sem, recv_sem=recv_sem, device_id=device, device_id_type=MESH
        )
        if cond is None:
            copy.start()
        else:
            pl.when(cond)(copy.start)
        self.pending.append((copy, cond))

    def drain(self):
        for copy, cond in self.pending:
            if cond is None:
                copy.wait_send()
            else:
                pl.when(cond)(copy.wait_send)
        self.pending = []


def arrived(ref, sem, device):
    pltpu.make_async_remote_copy(
        src_ref=ref, dst_ref=ref, send_sem=sem, recv_sem=sem, device_id=device, device_id_type=MESH
    ).wait_recv()


class Gather:
    def __init__(self, me, sends, own, slot, ssem, rsem):
        self.me, self.sends, self.own, self.slot, self.ssem, self.rsem = me, sends, own, slot, ssem, rsem

    def source(self, h, i, j):
        a, b = (i, j) if h == 0 else (j, i)
        return (self.me.x + self.me.sg * OFFSETS[a] + 8) % 4, (self.me.y + self.me.sg * OFFSETS[b] + 8) % 4

    def send(self, h, have, give, axis, sign):
        me = self.me
        px, py = self.source(h, *have)
        dst = self.slot(h, px, py)
        src = self.own(h) if have == (0, 0) else dst
        along_x = (axis == 0) == (h == 0)
        if along_x:
            device = me.at(x=(me.x + sign * me.sg + 4) % 4)
        else:
            device = me.at(y=(me.y + sign * me.sg + 4) % 4)
        k = h * 16 + give[0] * 4 + give[1]
        self.sends.start(src, dst, self.ssem.at[k], self.rsem.at[k], device)

    def begin(self, h):
        self.send(h, (0, 0), (1, 0), 0, 1)
        self.send(h, (0, 0), (2, 0), 0, -1)
        self.send(h, (0, 0), (0, 1), 1, 1)
        self.send(h, (0, 0), (0, 2), 1, -1)

    def event(self, h, i, j):
        px, py = self.source(h, i, j)
        arrived(self.slot(h, px, py), self.rsem.at[h * 16 + i * 4 + j], self.me.at(c=1 - self.me.c))
        if j == 0:
            if i == 1:
                self.send(h, (1, 0), (3, 0), 0, 1)
            self.send(h, (i, 0), (i, 1), 1, 1)
            self.send(h, (i, 0), (i, 2), 1, -1)
        elif j == 1:
            self.send(h, (i, 1), (i, 3), 1, 1)

    def level(self, n):
        for i, j in LEVELS[n]:
            for h in (0, 1):
                self.event(h, i, j)


def kernel(
    ctx, w, res, fin, gram, cross,
    wbuf, cbuf, rbuf, part, mine_out, other, fbuf, sbuf, lbuf,
    w_s, w_r, f_s, f_r, s_s, s_r, a_s, a_r, z_s, z_r, b_s, b_r, e_s, e_r, x_s, x_r, t_s, t_r, l_s, l_r, own_sem,
):
    me = Place()
    sends = Sends()
    sibling = me.at(c=1 - me.c)
    partner = me.at(zh=1 - me.zh)
    lead = me.x // 2
    root = 2 * me.y + me.zh
    on_line = me.c == lead
    is_root = on_line & (me.zl == root)
    feeds = me.zl % 2 == me.zh
    other_core = 1 - me.c
    to_core, from_core = me.q // 8, me.x // 2
    swaps_self = (me.x // 2 == me.c) & (me.q // 8 == me.c)

    own_w = pltpu.make_async_copy(w, wbuf.at[me.q], own_sem.at[0])
    own_w.start()
    own_f = pltpu.make_async_copy(fin, fbuf.at[me.zh, me.y, pl.ds(4 * me.x, 4)], own_sem.at[1])
    own_f.start()

    barrier = pltpu.get_barrier_semaphore()

    def greet(device, cond=None):
        signal = lambda: pl.semaphore_signal(barrier, inc=1, device_id=device, device_id_type=MESH)
        if cond is None:
            signal()
        else:
            pl.when(cond)(signal)

    for k in (1, 2, 3):
        greet(me.at(y=(me.y + k) % 4))
    for k in (1, 3):
        greet(me.at(x=(me.x + k) % 4))
    for k in range(1, 8):
        greet(me.at(zl=(me.zl + k) % 8))
    greet(partner)
    greet(sibling)
    for i in range(8):
        p = 8 * me.c + i
        greet(me.at(y=p // 4, x=p % 4, c=from_core), jnp.logical_not((p == me.q) & (from_core == me.c)))

    @pl.when(is_root)
    def _():
        for k in range(1, 16):
            p = (me.q + k) % 16
            greet(me.at(y=p // 4, x=p % 4))

    here = feeds & (me.y == me.zl // 2) & (me.x // 2 == me.c)
    count = 3 + 2 + 7 + 1 + 1 + 8 - jnp.where(swaps_self, 1, 0) + jnp.where(feeds, 2, 0) - jnp.where(here, 1, 0)
    pl.semaphore_wait(barrier, count)

    slot_of = lambda zl: (zl % 2) * 4 + zl // 2
    lanes = pl.ds(pl.multiple_of(me.q * 256, 256), 256)
    for i in range(8):
        px, py = 2 * me.c + i // 4, i % 4
        src, dst = ctx.at[pl.ds(16 * i, 16)], cbuf.at[slot_of(me.zl), :, lanes]
        k = me.q % 8
        mine = (px == me.x) & (py == me.y) & (to_core == me.c)
        sends.start(src, dst, a_s.at[i], a_r.at[k], me.at(y=py, x=px, c=to_core), cond=jnp.logical_not(mine))
        pl.when(mine)(pltpu.make_async_copy(src, dst, a_r.at[k]).start)

    gather_w = Gather(
        me, sends,
        lambda h: w.at[pl.ds(128 * h, 128)],
        lambda h, px, py: wbuf.at[py * 4 + px, pl.ds(128 * h, 128)],
        w_s, w_r,
    )
    gather_w.begin(0)
    gather_w.begin(1)
    sends.start(fin, fbuf.at[me.zh, me.y, pl.ds(4 * me.x, 4)], x_s.at[0], x_r.at[0], partner)

    for k in range(4):
        j = (me.y + k) % 4
        if k == 0:
            pltpu.make_async_copy(res.at[j], rbuf.at[me.y], e_r.at[0]).start()
        else:
            sends.start(res.at[j], rbuf.at[me.y], e_s.at[k], e_r.at[k], me.at(y=j))

    half = pl.ds(pl.multiple_of(me.c * 2048, 2048), 2048)
    other_half = pl.ds(pl.multiple_of(other_core * 2048, 2048), 2048)
    for i in range(8):
        piece = cbuf.at[slot_of(me.zl), :, pl.ds(pl.multiple_of((me.c * 8 + i) * 256, 256), 256)]
        arrived(piece, a_r.at[i], sibling)

    base, pos = (me.zl // 4) * 4, me.zl % 4
    far = (me.zl + 4) % 8
    line = lambda zl: cbuf.at[slot_of(zl), :, half]
    sends.start(line(me.zl), line(me.zl), z_s.at[4], z_r.at[4], me.at(zl=far))
    for k in (1, 2, 3):
        sends.start(line(me.zl), line(me.zl), z_s.at[k], z_r.at[k], me.at(zl=base + (pos + k) % 4))
    sends.start(line(me.zl), line(me.zl), b_s.at[0], b_r.at[0], sibling)

    def from_z(k):
        zl = far if k == 4 else base + (pos - k) % 4 if k < 4 else (4 - base) + (pos - (k - 4)) % 4
        return zl

    def along_z(k):
        piece = line(from_z(k))
        arrived(piece, z_r.at[k], sibling)
        if k == 4:
            for i in (1, 2, 3):
                sends.start(piece, piece, z_s.at[4 + i], z_r.at[4 + i], me.at(zl=base + (pos + i) % 4))
        sends.start(piece, piece, b_s.at[k], b_r.at[k], sibling)

    gather_w.level(0)
    along_z(4)
    along_z(1)
    along_z(3)
    along_z(2)
    gather_w.level(1)
    for k in (5, 7, 6):
        along_z(k)
    gather_w.level(2)
    arrived(fbuf.at[1 - me.zh, me.y, pl.ds(4 * me.x, 4)], x_r.at[0], sibling)
    own_f.wait()
    fslot = lambda h, px, py: fbuf.at[(me.zh + h) % 2, py, pl.ds(4 * px, 4)]
    gather_f = Gather(me, sends, lambda h: fslot(h, me.x, me.y), fslot, f_s, f_r)
    gather_f.begin(0)
    gather_f.begin(1)
    gather_w.level(3)
    for k in range(8):
        zl = me.zl if k == 0 else from_z(k)
        arrived(cbuf.at[slot_of(zl), :, other_half], b_r.at[k], sibling)
    own_w.wait()

    part[...] = jnp.zeros_like(part)

    def project(k, carry):
        cols = pl.ds(pl.multiple_of(k * 512, 512), 512)
        a = cbuf[:, :, cols].reshape(128, 512)
        b = wbuf[pl.ds(2 * k, 2)].reshape(512, 512)
        part[...] += jnp.dot(a, b, preferred_element_type=jnp.float32).reshape(8, 16, 512)
        return carry

    lax.fori_loop(0, 8, project, 0)
    for k in range(4):
        arrived(rbuf.at[(me.y - k) % 4], e_r.at[k], sibling)
    mine = pl.ds(4 * me.zh, 4)
    part[mine] = part[mine] + rbuf[...].astype(jnp.float32)
    mine_out[...] = part[...].astype(jnp.bfloat16)
    for h in (0, 1):
        rows = pl.ds(4 * h, 4)
        sends.start(mine_out.at[rows], other.at[rows], x_s.at[1 + h], x_r.at[1 + h], partner)
    for n in range(4):
        gather_f.level(n)

    sslot = lambda h, px, py: sbuf.at[pl.ds(4 * h, 4), px * 4 + py]
    gather_s = Gather(me, sends, lambda h: sslot(h, me.x, me.y), sslot, s_s, s_r)
    for h in (0, 1):
        rows = pl.ds(4 * h, 4)
        arrived(other.at[rows], x_r.at[1 + h], sibling)
        sbuf[rows, me.n] = (part[rows] + other[rows].astype(jnp.float32)).astype(jnp.bfloat16)
        for j in (0, 1):
            px = 2 * me.c + j
            self_here = feeds & (me.y == me.zl // 2) & (me.x == px)
            src, dst = sbuf.at[rows, me.n, :, pl.ds(256 * j, 256)], lbuf.at[rows, me.n]
            sem = t_r.at[h * 16 + me.n]
            sends.start(
                src, dst, t_s.at[h * 2 + j], sem, me.at(y=me.zl // 2, x=px), cond=feeds & jnp.logical_not(self_here)
            )
            pl.when(self_here)(pltpu.make_async_copy(src, dst, sem).start)
        gather_s.begin(h)

    fed = on_line & (me.zl != root)
    above, below = me.zl > root, me.zl < root
    up_hop, down_hop = (8 - root) // 2, (root + 1) // 2
    o_up, o_down = me.zl - root, root - me.zl
    has_up = on_line & (
        ((me.zl == root) & (root < 7))
        | (above & (o_up >= up_hop) & (me.zl < 7))
        | (below & (o_down <= down_hop) & (o_down > 1))
    )
    has_down = on_line & (
        ((me.zl == root) & (root > 0))
        | (below & (o_down >= down_hop) & (me.zl > 0))
        | (above & (o_up <= up_hop) & (o_up > 1))
    )
    at_root = jnp.where(me.zl == root, 1, 0)
    up_zl = jnp.minimum(me.zl + at_root * up_hop + (1 - at_root), 7)
    down_zl = jnp.maximum(me.zl - at_root * down_hop - (1 - at_root), 0)

    def message(m):
        return lbuf.at[pl.ds(4 * (m // 8), 4), pl.ds(2 * (m % 8), 2)]

    def pass_on(m, who):
        piece = message(m)
        sends.start(piece, piece, l_s.at[m], l_r.at[m], me.at(zl=up_zl), cond=has_up & who)
        sends.start(piece, piece, l_s.at[16 + m], l_r.at[m], me.at(zl=down_zl), cond=has_down & who)
        sends.start(piece, piece, l_s.at[32 + m], l_r.at[16 + m], sibling, cond=who)

    def root_sends(m):
        h, g = m // 8, m % 8

        @pl.when(is_root)
        def _():
            for n in (2 * g, 2 * g + 1):
                arrived(lbuf.at[pl.ds(4 * h, 4), n], t_r.at[h * 16 + n], sibling)

        pass_on(m, is_root)

    def take(m):
        pl.when(fed)(lambda: arrived(message(m), l_r.at[m], sibling))
        pass_on(m, fed)
        pl.when(jnp.logical_not(on_line))(lambda: arrived(message(m), l_r.at[16 + m], sibling))

    gather_s.level(0)
    for m in range(8):
        root_sends(m)
    gather_s.level(1)
    for m in range(8, 16):
        root_sends(m)
    for m in range(8):
        take(m)
    gather_s.level(2)
    gather_s.level(3)

    gram[...] = jnp.zeros_like(gram)
    cross[...] = jnp.zeros_like(cross)

    def add(g):
        pair = pl.ds(2 * g, 2)
        a = lbuf[:, pair].reshape(256, 256)
        s = sbuf[:, pair].reshape(256, 512)
        f = fbuf[:, :, pair].reshape(256, 512)
        dims = (((0,), (0,)), ((), ()))
        gram[...] += lax.dot_general(a, s, dims, preferred_element_type=jnp.float32)
        cross[...] += lax.dot_general(a, f, dims, preferred_element_type=jnp.float32)

    for g in range(8):
        take(8 + g)
        add(g)
    gram[...] = gram[...] * (1.0 / 2048)
    cross[...] = cross[...] * (1.0 / 2048)
    sends.drain()


def body(context, out_weight, residual, final_states):
    vmem, hbm = pl.BlockSpec(memory_space=pltpu.VMEM), pl.BlockSpec(memory_space=pl.ANY)
    dma = lambda n: pltpu.SemaphoreType.DMA((n,))
    bf16, f32 = jnp.bfloat16, jnp.float32
    out = jax.ShapeDtypeStruct((256, 512), f32)
    return pl.pallas_call(
        kernel,
        out_shape=(out, out),
        in_specs=[hbm] * 4,
        out_specs=(vmem, vmem),
        scratch_shapes=[
            pltpu.VMEM((16, 256, 512), bf16),
            pltpu.VMEM((8, 16, 4096), bf16),
            pltpu.VMEM((4, 16, 512), bf16),
            pltpu.VMEM((8, 16, 512), f32),
            pltpu.VMEM((8, 16, 512), bf16),
            pltpu.VMEM((8, 16, 512), bf16),
            pltpu.VMEM((2, 4, 16, 16, 512), bf16),
            pltpu.VMEM((8, 16, 16, 512), bf16),
            pltpu.VMEM((8, 16, 16, 256), bf16),
            dma(32), dma(32), dma(32), dma(32), dma(32), dma(32),
            dma(8), dma(8), dma(8), dma(8), dma(8), dma(8),
            dma(4), dma(4), dma(3), dma(3), dma(4), dma(32), dma(48), dma(32), dma(2),
        ],
        compiler_params=pltpu.CompilerParams(collective_id=0, has_side_effects=True, vmem_limit_bytes=56 << 20),
        cost_estimate=pl.CostEstimate(flops=1 << 31, bytes_accessed=1 << 21, transcendentals=0),
    )(context, out_weight, residual.reshape(4, 16, 512), final_states.reshape(4, 16, 512))


def solution(mesh):
    in_specs = (P("tensor", "dp"), P("dp", "tensor"), P("dp", "tensor"), P("dp", "tensor"))
    out_specs = (P("dp", "tensor"), P("dp", "tensor"))
    return jax.shard_map(body, mesh=mesh, in_specs=in_specs, out_specs=out_specs, check_vma=False)
```

time: 127 us -> 112 us (0.88)
  the two profiles are of different devices: /device:TPU:25 before, /device:TPU:33 now
where the time goes in v2:
time: 112 us
  Pallas kernels  109 us (97%)
  local copies, waits for them, and re-layouts  2.72 us (2%)
    pallas_call x1, Pallas kernels, body(): pl.pallas_call(kernel, out_shape=(out, out), in_specs=[hbm] * 4, out_spec...  109 us
    unnamed x4, local copies, waits for them, and re-layouts  2.72 us

profile of v2, /device:TPU:33, one launch (start us, length us, event | category | flops | bytes accessed | tf_op | source)
XLA Modules:
  0.0 112.2 jit_solution(3916548983245522619)
XLA Ops:
  0.6 108.8 %shard_map.59 = (f32[256,512]{1,0:T(8,128)}, f32[256,512]{1,0:T(8,128)}) custom-call(bf16[128,256]{1,0:T(8,128)(2,1)} %ctx.1, bf16[256,512]{1,0:T(8,128)(2,1)} %w.1, bf16[4,16,512]{2,1,0:T(8,128)(2,1)} %bitcast.2, bf16[4,16,512]{2,1,0:T(8,128)(2,1)} %bitcast.3), custom_call_target="tpu_custom_call" | custom-call | flops 2147483648 | bytes 2097152 | tf_op jit(solution)/shard_map/pallas_call | solution.py:347
  109.5 0.0 copy-start
  109.5 1.9 %copy.8 = f32[256,512]{1,0:T(8,128)} copy(f32[256,512]{1,0:T(8,128)} %get-tuple-element.4) | data formatting | bytes 1048576
  111.4 0.0 copy-done
  111.4 0.8 copy.9
Async XLA Ops:
  109.5 1.9 %copy-start = (f32[256,512]{1,0:T(8,128)S(1)}, f32[256,512]{1,0:T(8,128)}, u32[]{:S(2)}) copy-start(f32[256,512]{1,0:T(8,128)} %get-tuple-element.5) | copy-start | bytes 1572868

commit v3 on v2

--- a/solution.py
+++ b/solution.py
@@ -7,12 +7,12 @@
 
 MESH = pl.DeviceIdType.MESH
 OFFSETS = (0, -1, 1, -2)
-LEVELS = (
-    ((1, 0), (2, 0), (0, 1), (0, 2)),
-    ((3, 0), (1, 1), (2, 1), (1, 2), (2, 2), (0, 3)),
-    ((3, 1), (3, 2), (1, 3), (2, 3)),
-    ((3, 3),),
-)
+LEVELS = (((1, 0), (2, 0), (0, 1)), ((3, 0), (1, 1), (2, 1)), ((3, 1),))
+LAST = ((0, 2), (1, 2), (2, 2), (0, 3), (3, 2), (1, 3), (2, 3), (3, 3))
+EARLY = ((0, 0), (1, 0), (0, 1), (2, 0), (0, 2), (1, 1), (1, 2), (2, 1), (2, 2), (3, 0), (0, 3))
+LATE = ((3, 1), (1, 3), (3, 2), (2, 3), (3, 3))
+
+
 class Place:
     def __init__(self):
         d, t = lax.axis_index("dp"), lax.axis_index("tensor")
@@ -61,7 +61,7 @@
         self.me, self.sends, self.own, self.slot, self.ssem, self.rsem = me, sends, own, slot, ssem, rsem
 
     def source(self, h, i, j):
-        a, b = (i, j) if h == 0 else (j, i)
+        a, b = (i, j) if h % 2 == 0 else (j, i)
         return (self.me.x + self.me.sg * OFFSETS[a] + 8) % 4, (self.me.y + self.me.sg * OFFSETS[b] + 8) % 4
 
     def send(self, h, have, give, axis, sign):
@@ -69,7 +69,7 @@
         px, py = self.source(h, *have)
         dst = self.slot(h, px, py)
         src = self.own(h) if have == (0, 0) else dst
-        along_x = (axis == 0) == (h == 0)
+        along_x = (axis == 0) == (h % 2 == 0)
         if along_x:
             device = me.at(x=(me.x + sign * me.sg + 4) % 4)
         else:
@@ -94,9 +94,14 @@
         elif j == 1:
             self.send(h, (i, 1), (i, 3), 1, 1)
 
-    def level(self, n):
+    def level(self, n, parts=(0, 1)):
         for i, j in LEVELS[n]:
-            for h in (0, 1):
+            for h in parts:
+                self.event(h, i, j)
+
+    def finish(self, parts=(0, 1), which=LAST):
+        for i, j in which:
+            for h in parts:
                 self.event(h, i, j)
 
 
@@ -183,6 +188,7 @@
 
     half = pl.ds(pl.multiple_of(me.c * 2048, 2048), 2048)
     other_half = pl.ds(pl.multiple_of(other_core * 2048, 2048), 2048)
+    gather_w.level(0)
     for i in range(8):
         piece = cbuf.at[slot_of(me.zl), :, pl.ds(pl.multiple_of((me.c * 8 + i) * 256, 256), 256)]
         arrived(piece, a_r.at[i], sibling)
@@ -207,13 +213,8 @@
                 sends.start(piece, piece, z_s.at[4 + i], z_r.at[4 + i], me.at(zl=base + (pos + i) % 4))
         sends.start(piece, piece, b_s.at[k], b_r.at[k], sibling)
 
-    gather_w.level(0)
-    along_z(4)
-    along_z(1)
-    along_z(3)
-    along_z(2)
     gather_w.level(1)
-    for k in (5, 7, 6):
+    for k in (4, 1, 3, 2):
         along_z(k)
     gather_w.level(2)
     arrived(fbuf.at[1 - me.zh, me.y, pl.ds(4 * me.x, 4)], x_r.at[0], sibling)
@@ -222,49 +223,53 @@
     gather_f = Gather(me, sends, lambda h: fslot(h, me.x, me.y), fslot, f_s, f_r)
     gather_f.begin(0)
     gather_f.begin(1)
-    gather_w.level(3)
+    for k in (5, 7, 6):
+        along_z(k)
     for k in range(8):
         zl = me.zl if k == 0 else from_z(k)
         arrived(cbuf.at[slot_of(zl), :, other_half], b_r.at[k], sibling)
     own_w.wait()
 
-    part[...] = jnp.zeros_like(part)
-
-    def project(k, carry):
-        cols = pl.ds(pl.multiple_of(k * 512, 512), 512)
-        a = cbuf[:, :, cols].reshape(128, 512)
-        b = wbuf[pl.ds(2 * k, 2)].reshape(512, 512)
-        part[...] += jnp.dot(a, b, preferred_element_type=jnp.float32).reshape(8, 16, 512)
-        return carry
-
-    lax.fori_loop(0, 8, project, 0)
+    def project(sources):
+        total = None
+        for i, j in sources:
+            px, py = gather_w.source(0, i, j)
+            k = py * 4 + px
+            a = cbuf[:, :, pl.ds(pl.multiple_of(k * 256, 256), 256)].reshape(128, 256)
+            new = jnp.dot(a, wbuf[k], preferred_element_type=jnp.float32)
+            total = new if total is None else total + new
+        return total.reshape(8, 16, 512)
+
+    gather_w.finish((0, 1), LAST[:4])
+    part[...] = project(EARLY)
+    gather_w.finish((0, 1), LAST[4:])
+    part[...] += project(LATE)
     for k in range(4):
         arrived(rbuf.at[(me.y - k) % 4], e_r.at[k], sibling)
     mine = pl.ds(4 * me.zh, 4)
     part[mine] = part[mine] + rbuf[...].astype(jnp.float32)
     mine_out[...] = part[...].astype(jnp.bfloat16)
-    for h in (0, 1):
-        rows = pl.ds(4 * h, 4)
-        sends.start(mine_out.at[rows], other.at[rows], x_s.at[1 + h], x_r.at[1 + h], partner)
-    for n in range(4):
-        gather_f.level(n)
-
-    sslot = lambda h, px, py: sbuf.at[pl.ds(4 * h, 4), px * 4 + py]
-    gather_s = Gather(me, sends, lambda h: sslot(h, me.x, me.y), sslot, s_s, s_r)
-    for h in (0, 1):
-        rows = pl.ds(4 * h, 4)
-        arrived(other.at[rows], x_r.at[1 + h], sibling)
+    for k in range(4):
+        rows = pl.ds(2 * k, 2)
+        sends.start(mine_out.at[rows], other.at[rows], x_s.at[1 + k], x_r.at[1 + k], partner)
+
+    sslot = lambda k, px, py: sbuf.at[pl.ds(2 * k, 2), px * 4 + py]
+    gather_s = Gather(me, sends, lambda k: sslot(k, me.x, me.y), sslot, s_s, s_r)
+
+    def share(k):
+        rows = pl.ds(2 * k, 2)
+        arrived(other.at[rows], x_r.at[1 + k], sibling)
         sbuf[rows, me.n] = (part[rows] + other[rows].astype(jnp.float32)).astype(jnp.bfloat16)
         for j in (0, 1):
             px = 2 * me.c + j
             self_here = feeds & (me.y == me.zl // 2) & (me.x == px)
             src, dst = sbuf.at[rows, me.n, :, pl.ds(256 * j, 256)], lbuf.at[rows, me.n]
-            sem = t_r.at[h * 16 + me.n]
+            sem = t_r.at[k * 16 + me.n]
             sends.start(
-                src, dst, t_s.at[h * 2 + j], sem, me.at(y=me.zl // 2, x=px), cond=feeds & jnp.logical_not(self_here)
+                src, dst, t_s.at[k * 2 + j], sem, me.at(y=me.zl // 2, x=px), cond=feeds & jnp.logical_not(self_here)
             )
             pl.when(self_here)(pltpu.make_async_copy(src, dst, sem).start)
-        gather_s.begin(h)
+        gather_s.begin(k)
 
     fed = on_line & (me.zl != root)
     above, below = me.zl > root, me.zl < root
@@ -284,58 +289,89 @@
     up_zl = jnp.minimum(me.zl + at_root * up_hop + (1 - at_root), 7)
     down_zl = jnp.maximum(me.zl - at_root * down_hop - (1 - at_root), 0)
 
+    depth = jnp.where(above, 1 + jnp.abs(o_up - up_hop), jnp.where(below, 1 + jnp.abs(o_down - down_hop), 0))
+
     def message(m):
-        return lbuf.at[pl.ds(4 * (m // 8), 4), pl.ds(2 * (m % 8), 2)]
-
-    def pass_on(m, who):
-        piece = message(m)
-        sends.start(piece, piece, l_s.at[m], l_r.at[m], me.at(zl=up_zl), cond=has_up & who)
-        sends.start(piece, piece, l_s.at[16 + m], l_r.at[m], me.at(zl=down_zl), cond=has_down & who)
-        sends.start(piece, piece, l_s.at[32 + m], l_r.at[16 + m], sibling, cond=who)
-
-    def root_sends(m):
-        h, g = m // 8, m % 8
-
+        return lbuf.at[pl.ds(2 * (m // 4), 2), pl.ds(4 * (m % 4), 4)]
+
+    def forwards(m):
+        def copy(send, recv, device):
+            return pltpu.make_async_remote_copy(
+                src_ref=message(m), dst_ref=message(m), send_sem=l_s.at[send], recv_sem=l_r.at[recv],
+                device_id=device, device_id_type=MESH,
+            )
+
+        up, down = copy(m, m, me.at(zl=up_zl)), copy(16 + m, m, me.at(zl=down_zl))
+        return (up, has_up), (down, has_down), (copy(32 + m, 16 + m, sibling), on_line)
+
+    def pass_on(m):
+        for copy, cond in forwards(m):
+            pl.when(cond)(copy.start)
+
+    def root_sends(k):
         @pl.when(is_root)
         def _():
-            for n in (2 * g, 2 * g + 1):
-                arrived(lbuf.at[pl.ds(4 * h, 4), n], t_r.at[h * 16 + n], sibling)
-
-        pass_on(m, is_root)
-
-    def take(m):
-        pl.when(fed)(lambda: arrived(message(m), l_r.at[m], sibling))
-        pass_on(m, fed)
-        pl.when(jnp.logical_not(on_line))(lambda: arrived(message(m), l_r.at[16 + m], sibling))
-
-    gather_s.level(0)
-    for m in range(8):
-        root_sends(m)
-    gather_s.level(1)
-    for m in range(8, 16):
-        root_sends(m)
-    for m in range(8):
-        take(m)
-    gather_s.level(2)
-    gather_s.level(3)
-
-    gram[...] = jnp.zeros_like(gram)
-    cross[...] = jnp.zeros_like(cross)
-
-    def add(g):
-        pair = pl.ds(2 * g, 2)
-        a = lbuf[:, pair].reshape(256, 256)
-        s = sbuf[:, pair].reshape(256, 512)
-        f = fbuf[:, :, pair].reshape(256, 512)
+            for u in range(4):
+                for n in range(4 * u, 4 * u + 4):
+                    arrived(lbuf.at[pl.ds(2 * k, 2), n], t_r.at[k * 16 + n], sibling)
+                pass_on(4 * k + u)
+
+    def take(k, d):
+        @pl.when(on_line & (depth == d))
+        def _():
+            for m in range(4 * k, 4 * k + 4):
+                arrived(message(m), l_r.at[m], sibling)
+                pass_on(m)
+
+    def from_sibling(k):
+        @pl.when(jnp.logical_not(on_line))
+        def _():
+            for m in range(4 * k, 4 * k + 4):
+                arrived(message(m), l_r.at[16 + m], sibling)
+
+    def add(first, parts):
+        rows = pl.ds(2 * first, 2 * parts)
+        depth_of = parts * 512
+        a = lbuf[rows].reshape(depth_of, 256)
+        f = fbuf[first // 2, pl.ds(2 * (first % 2), 2 * parts)]
         dims = (((0,), (0,)), ((), ()))
-        gram[...] += lax.dot_general(a, s, dims, preferred_element_type=jnp.float32)
-        cross[...] += lax.dot_general(a, f, dims, preferred_element_type=jnp.float32)
-
-    for g in range(8):
-        take(8 + g)
-        add(g)
-    gram[...] = gram[...] * (1.0 / 2048)
-    cross[...] = cross[...] * (1.0 / 2048)
+        for out, buf in ((gram, sbuf[rows]), (cross, f)):
+            new = lax.dot_general(a, buf.reshape(depth_of, 512), dims, preferred_element_type=jnp.float32) * (1.0 / 2048)
+            out[...] = new if first == 0 else out[...] + new
+
+    for slot in range(9):
+        if slot == 0:
+            gather_f.level(0)
+            gather_f.level(1)
+        if slot == 1:
+            gather_f.level(2)
+        if slot < 4:
+            share(slot)
+        for n in range(3):
+            k = slot - 1 - n
+            if 0 <= k < 4:
+                gather_s.level(n, (k,))
+        if 0 <= slot - 1 < 4:
+            root_sends(slot - 1)
+        for d in range(1, 5):
+            k = slot - 1 - d
+            if 0 <= k < 4:
+                if (k, d) == (3, 4):
+                    gather_f.finish()
+                    gather_s.finish((0, 1))
+                    from_sibling(0)
+                    from_sibling(1)
+                    add(0, 2)
+                    gather_s.finish((2,))
+                    from_sibling(2)
+                    add(2, 1)
+                take(k, d)
+    gather_s.finish((3,))
+    from_sibling(3)
+    add(3, 1)
+    for m in range(16):
+        for copy, cond in forwards(m):
+            pl.when(cond)(copy.wait_send)
     sends.drain()
 
 
@@ -359,9 +395,9 @@
             pltpu.VMEM((2, 4, 16, 16, 512), bf16),
             pltpu.VMEM((8, 16, 16, 512), bf16),
             pltpu.VMEM((8, 16, 16, 256), bf16),
-            dma(32), dma(32), dma(32), dma(32), dma(32), dma(32),
+            dma(32), dma(32), dma(32), dma(32), dma(64), dma(64),
             dma(8), dma(8), dma(8), dma(8), dma(8), dma(8),
-            dma(4), dma(4), dma(3), dma(3), dma(4), dma(32), dma(48), dma(32), dma(2),
+            dma(4), dma(4), dma(5), dma(5), dma(8), dma(64), dma(48), dma(32), dma(2),
         ],
         compiler_params=pltpu.CompilerParams(collective_id=0, has_side_effects=True, vmem_limit_bytes=56 << 20),
         cost_estimate=pl.CostEstimate(flops=1 << 31, bytes_accessed=1 << 21, transcendentals=0),

time: 112 us -> 96.8 us (0.86)
  Pallas kernels: 109 us -> 93.3 us
    pallas_call x1, Pallas kernels: 109 us -> 93.3 us  [body(): pl.pallas_call(kernel, out_shape=(out, out), in_specs=[hbm] * 4, out_spec...]
where the time goes in v3:
time: 96.8 us; the launch traced here: 96.6 us
  Pallas kernels  93.3 us (96%)
  local copies, waits for them, and re-layouts  2.72 us (3%)
    pallas_call x1, Pallas kernels, body(): pl.pallas_call(kernel, out_shape=(out, out), in_specs=[hbm] * 4, out_spec...  93.3 us
    unnamed x4, local copies, waits for them, and re-layouts  2.72 us

profile of v3, /device:TPU:33, one launch (start us, length us, event | category | flops | bytes accessed | tf_op | source)
XLA Modules:
  0.0 96.6 jit_solution(11151555169020263381)
XLA Ops:
  0.6 93.3 %shard_map.59 = (f32[256,512]{1,0:T(8,128)}, f32[256,512]{1,0:T(8,128)}) custom-call(bf16[128,256]{1,0:T(8,128)(2,1)} %ctx.1, bf16[256,512]{1,0:T(8,128)(2,1)} %w.1, bf16[4,16,512]{2,1,0:T(8,128)(2,1)} %bitcast.2, bf16[4,16,512]{2,1,0:T(8,128)(2,1)} %bitcast.3), custom_call_target="tpu_custom_call" | custom-call | flops 2147483648 | bytes 2097152 | tf_op jit(solution)/shard_map/pallas_call | solution.py:383
  93.9 0.0 copy-start
  93.9 1.9 %copy.8 = f32[256,512]{1,0:T(8,128)} copy(f32[256,512]{1,0:T(8,128)} %get-tuple-element.4) | data formatting | bytes 1048576
  95.8 0.0 copy-done
  95.9 0.8 copy.9
Async XLA Ops:
  93.9 1.9 %copy-start = (f32[256,512]{1,0:T(8,128)S(1)}, f32[256,512]{1,0:T(8,128)}, u32[]{:S(2)}) copy-start(f32[256,512]{1,0:T(8,128)} %get-tuple-element.5) | copy-start | bytes 1572868

commit v4 on v3

--- a/solution.py
+++ b/solution.py
@@ -107,17 +107,15 @@
 
 def kernel(
     ctx, w, res, fin, gram, cross,
-    wbuf, cbuf, rbuf, part, mine_out, other, fbuf, sbuf, lbuf,
-    w_s, w_r, f_s, f_r, s_s, s_r, a_s, a_r, z_s, z_r, b_s, b_r, e_s, e_r, x_s, x_r, t_s, t_r, l_s, l_r, own_sem,
+    wbuf, cbuf, rbuf, part, mine_out, other, fbuf, sbuf, zbuf, lbuf,
+    w_s, w_r, f_s, f_r, s_s, s_r, a_s, a_r, z_s, z_r, b_s, b_r, e_s, e_r, x_s, x_r, t_s, t_r, u_s, u_r, l_s, l_r, own_sem,
 ):
     me = Place()
     sends = Sends()
     sibling = me.at(c=1 - me.c)
     partner = me.at(zh=1 - me.zh)
     lead = me.x // 2
-    root = 2 * me.y + me.zh
     on_line = me.c == lead
-    is_root = on_line & (me.zl == root)
     feeds = me.zl % 2 == me.zh
     other_core = 1 - me.c
     to_core, from_core = me.q // 8, me.x // 2
@@ -141,22 +139,22 @@
         greet(me.at(y=(me.y + k) % 4))
     for k in (1, 3):
         greet(me.at(x=(me.x + k) % 4))
-    for k in range(1, 8):
-        greet(me.at(zl=(me.zl + k) % 8))
+    for k in (1, 2, 3):
+        greet(me.at(zl=(me.zl // 4) * 4 + (me.zl + k) % 4))
+    greet(me.at(zl=(me.zl + 4) % 8))
     greet(partner)
     greet(sibling)
     for i in range(8):
         p = 8 * me.c + i
         greet(me.at(y=p // 4, x=p % 4, c=from_core), jnp.logical_not((p == me.q) & (from_core == me.c)))
 
-    @pl.when(is_root)
+    @pl.when(on_line)
     def _():
         for k in range(1, 16):
             p = (me.q + k) % 16
             greet(me.at(y=p // 4, x=p % 4))
 
-    here = feeds & (me.y == me.zl // 2) & (me.x // 2 == me.c)
-    count = 3 + 2 + 7 + 1 + 1 + 8 - jnp.where(swaps_self, 1, 0) + jnp.where(feeds, 2, 0) - jnp.where(here, 1, 0)
+    count = 3 + 2 + 4 + 1 + 1 + 8 - jnp.where(swaps_self, 1, 0) + 8 - jnp.where(on_line, 1, 0)
     pl.semaphore_wait(barrier, count)
 
     slot_of = lambda zl: (zl % 2) * 4 + zl // 2
@@ -259,75 +257,48 @@
     def share(k):
         rows = pl.ds(2 * k, 2)
         arrived(other.at[rows], x_r.at[1 + k], sibling)
-        sbuf[rows, me.n] = (part[rows] + other[rows].astype(jnp.float32)).astype(jnp.bfloat16)
-        for j in (0, 1):
-            px = 2 * me.c + j
-            self_here = feeds & (me.y == me.zl // 2) & (me.x == px)
-            src, dst = sbuf.at[rows, me.n, :, pl.ds(256 * j, 256)], lbuf.at[rows, me.n]
-            sem = t_r.at[k * 16 + me.n]
-            sends.start(
-                src, dst, t_s.at[k * 2 + j], sem, me.at(y=me.zl // 2, x=px), cond=feeds & jnp.logical_not(self_here)
-            )
-            pl.when(self_here)(pltpu.make_async_copy(src, dst, sem).start)
+        new = (part[rows] + other[rows].astype(jnp.float32)).astype(jnp.bfloat16)
+        sbuf[rows, me.n] = new
+
+        @pl.when(feeds)
+        def _():
+            zbuf[me.zl // 2, rows] = new
+
+        piece = zbuf.at[me.zl // 2, rows]
+        recv = u_r.at[k * 4 + me.zl // 2]
+        sends.start(piece, piece, u_s.at[k * 7], recv, me.at(zl=far), cond=feeds)
+        for i in (1, 2, 3):
+            sends.start(piece, piece, u_s.at[k * 7 + i], recv, me.at(zl=base + (pos + i) % 4), cond=feeds)
         gather_s.begin(k)
 
-    fed = on_line & (me.zl != root)
-    above, below = me.zl > root, me.zl < root
-    up_hop, down_hop = (8 - root) // 2, (root + 1) // 2
-    o_up, o_down = me.zl - root, root - me.zl
-    has_up = on_line & (
-        ((me.zl == root) & (root < 7))
-        | (above & (o_up >= up_hop) & (me.zl < 7))
-        | (below & (o_down <= down_hop) & (o_down > 1))
-    )
-    has_down = on_line & (
-        ((me.zl == root) & (root > 0))
-        | (below & (o_down >= down_hop) & (me.zl > 0))
-        | (above & (o_up <= up_hop) & (o_up > 1))
-    )
-    at_root = jnp.where(me.zl == root, 1, 0)
-    up_zl = jnp.minimum(me.zl + at_root * up_hop + (1 - at_root), 7)
-    down_zl = jnp.maximum(me.zl - at_root * down_hop - (1 - at_root), 0)
-
-    depth = jnp.where(above, 1 + jnp.abs(o_up - up_hop), jnp.where(below, 1 + jnp.abs(o_down - down_hop), 0))
-
-    def message(m):
-        return lbuf.at[pl.ds(2 * (m // 4), 2), pl.ds(4 * (m % 4), 4)]
-
-    def forwards(m):
-        def copy(send, recv, device):
-            return pltpu.make_async_remote_copy(
-                src_ref=message(m), dst_ref=message(m), send_sem=l_s.at[send], recv_sem=l_r.at[recv],
-                device_id=device, device_id_type=MESH,
-            )
-
-        up, down = copy(m, m, me.at(zl=up_zl)), copy(16 + m, m, me.at(zl=down_zl))
-        return (up, has_up), (down, has_down), (copy(32 + m, 16 + m, sibling), on_line)
-
-    def pass_on(m):
-        for copy, cond in forwards(m):
-            pl.when(cond)(copy.start)
-
-    def root_sends(k):
-        @pl.when(is_root)
-        def _():
-            for u in range(4):
-                for n in range(4 * u, 4 * u + 4):
-                    arrived(lbuf.at[pl.ds(2 * k, 2), n], t_r.at[k * 16 + n], sibling)
-                pass_on(4 * k + u)
-
-    def take(k, d):
-        @pl.when(on_line & (depth == d))
-        def _():
-            for m in range(4 * k, 4 * k + 4):
-                arrived(message(m), l_r.at[m], sibling)
-                pass_on(m)
+    def pass_along_z(k):
+        piece = zbuf.at[far // 2, pl.ds(2 * k, 2)]
+        recv = u_r.at[k * 4 + far // 2]
+        pl.when(feeds)(lambda: arrived(piece, recv, sibling))
+        for i in (1, 2, 3):
+            sends.start(piece, piece, u_s.at[k * 7 + 3 + i], recv, me.at(zl=base + (pos + i) % 4), cond=feeds)
+
+    def swap(k):
+        rows = pl.ds(2 * k, 2)
+        for p in range(4):
+            had = feeds & ((me.zl // 2 == p) | (far // 2 == p))
+            pl.when(jnp.logical_not(had))(lambda: arrived(zbuf.at[p, rows], u_r.at[k * 4 + p], sibling))
+            for j in (0, 1):
+                px = 2 * me.c + j
+                here = (me.y == p) & (me.x == px)
+                src, dst = zbuf.at[p, rows, :, pl.ds(256 * j, 256)], lbuf.at[rows, me.n]
+                sends.start(
+                    src, dst, t_s.at[k * 8 + p * 2 + j], t_r.at[k], me.at(y=p, x=px), cond=jnp.logical_not(here)
+                )
+                pl.when(here)(pltpu.make_async_copy(src, dst, t_r.at[k]).start)
+
+    def to_sibling(k):
+        piece = lbuf.at[pl.ds(2 * k, 2)]
+        pl.when(on_line)(lambda: arrived(piece, t_r.at[k], sibling))
+        sends.start(piece, piece, l_s.at[k], l_r.at[k], sibling, cond=on_line)
 
     def from_sibling(k):
-        @pl.when(jnp.logical_not(on_line))
-        def _():
-            for m in range(4 * k, 4 * k + 4):
-                arrived(message(m), l_r.at[16 + m], sibling)
+        pl.when(jnp.logical_not(on_line))(lambda: arrived(lbuf.at[pl.ds(2 * k, 2)], l_r.at[k], sibling))
 
     def add(first, parts):
         rows = pl.ds(2 * first, 2 * parts)
@@ -352,26 +323,23 @@
             if 0 <= k < 4:
                 gather_s.level(n, (k,))
         if 0 <= slot - 1 < 4:
-            root_sends(slot - 1)
-        for d in range(1, 5):
-            k = slot - 1 - d
-            if 0 <= k < 4:
-                if (k, d) == (3, 4):
-                    gather_f.finish()
-                    gather_s.finish((0, 1))
-                    from_sibling(0)
-                    from_sibling(1)
-                    add(0, 2)
-                    gather_s.finish((2,))
-                    from_sibling(2)
-                    add(2, 1)
-                take(k, d)
+            pass_along_z(slot - 1)
+        if 0 <= slot - 2 < 4:
+            swap(slot - 2)
+        if 0 <= slot - 5 < 4:
+            to_sibling(slot - 5)
+        if slot == 7:
+            gather_f.finish()
+            gather_s.finish((0, 1))
+            from_sibling(0)
+            from_sibling(1)
+            add(0, 2)
+    gather_s.finish((2,))
+    from_sibling(2)
+    add(2, 1)
     gather_s.finish((3,))
     from_sibling(3)
     add(3, 1)
-    for m in range(16):
-        for copy, cond in forwards(m):
-            pl.when(cond)(copy.wait_send)
     sends.drain()
 
 
@@ -394,10 +362,11 @@
             pltpu.VMEM((8, 16, 512), bf16),
             pltpu.VMEM((2, 4, 16, 16, 512), bf16),
             pltpu.VMEM((8, 16, 16, 512), bf16),
+            pltpu.VMEM((4, 8, 16, 512), bf16),
             pltpu.VMEM((8, 16, 16, 256), bf16),
             dma(32), dma(32), dma(32), dma(32), dma(64), dma(64),
             dma(8), dma(8), dma(8), dma(8), dma(8), dma(8),
-            dma(4), dma(4), dma(5), dma(5), dma(8), dma(64), dma(48), dma(32), dma(2),
+            dma(4), dma(4), dma(5), dma(5), dma(32), dma(4), dma(28), dma(16), dma(4), dma(4), dma(2),
         ],
         compiler_params=pltpu.CompilerParams(collective_id=0, has_side_effects=True, vmem_limit_bytes=56 << 20),
         cost_estimate=pl.CostEstimate(flops=1 << 31, bytes_accessed=1 << 21, transcendentals=0),

time: 96.8 us -> 89.7 us (0.927)
  the two profiles are of different devices: /device:TPU:33 before, /device:TPU:25 now
where the time goes in v4:
time: 89.7 us; the launch traced here: 88.3 us
  Pallas kernels  85 us (95%)
  local copies, waits for them, and re-layouts  2.72 us (3%)
    pallas_call x1, Pallas kernels, body(): pl.pallas_call(kernel, out_shape=(out, out), in_specs=[hbm] * 4, out_spec...  85 us
    unnamed x4, local copies, waits for them, and re-layouts  2.72 us

profile of v4, /device:TPU:25, one launch (start us, length us, event | category | flops | bytes accessed | tf_op | source)
XLA Modules:
  0.0 88.3 jit_solution(14554980337332432338)
XLA Ops:
  0.6 85.0 %shard_map.59 = (f32[256,512]{1,0:T(8,128)}, f32[256,512]{1,0:T(8,128)}) custom-call(bf16[128,256]{1,0:T(8,128)(2,1)} %ctx.1, bf16[256,512]{1,0:T(8,128)(2,1)} %w.1, bf16[4,16,512]{2,1,0:T(8,128)(2,1)} %bitcast.2, bf16[4,16,512]{2,1,0:T(8,128)(2,1)} %bitcast.3), custom_call_target="tpu_custom_call" | custom-call | flops 2147483648 | bytes 2097152 | tf_op jit(solution)/shard_map/pallas_call | solution.py:351
  85.6 0.0 copy-start
  85.6 1.9 %copy.8 = f32[256,512]{1,0:T(8,128)} copy(f32[256,512]{1,0:T(8,128)} %get-tuple-element.4) | data formatting | bytes 1048576
  87.5 0.0 copy-done
  87.5 0.8 copy.9
Async XLA Ops:
  85.6 1.9 %copy-start = (f32[256,512]{1,0:T(8,128)S(1)}, f32[256,512]{1,0:T(8,128)}, u32[]{:S(2)}) copy-start(f32[256,512]{1,0:T(8,128)} %get-tuple-element.5) | copy-start | bytes 1572868

commit v5 on v4

--- a/solution.py
+++ b/solution.py
@@ -11,6 +11,14 @@
 LAST = ((0, 2), (1, 2), (2, 2), (0, 3), (3, 2), (1, 3), (2, 3), (3, 3))
 EARLY = ((0, 0), (1, 0), (0, 1), (2, 0), (0, 2), (1, 1), (1, 2), (2, 1), (2, 2), (3, 0), (0, 3))
 LATE = ((3, 1), (1, 3), (3, 2), (2, 3), (3, 3))
+
+
+TREES = {
+    0: {0: (5, 2, 1), 5: (7, 6, 4), 2: (3,)},
+    2: {2: (7, 3, 1), 7: (6, 5), 3: (4,), 1: (0,)},
+    4: {4: (1, 3, 6, 5), 1: (0,), 3: (2,), 6: (7,)},
+    6: {6: (1, 4, 5, 7), 1: (0, 2), 4: (3,)},
+}
 
 
 class Place:
@@ -119,7 +127,6 @@
     feeds = me.zl % 2 == me.zh
     other_core = 1 - me.c
     to_core, from_core = me.q // 8, me.x // 2
-    swaps_self = (me.x // 2 == me.c) & (me.q // 8 == me.c)
 
     own_w = pltpu.make_async_copy(w, wbuf.at[me.q], own_sem.at[0])
     own_w.start()
@@ -135,18 +142,10 @@
         else:
             pl.when(cond)(signal)
 
-    for k in (1, 2, 3):
-        greet(me.at(y=(me.y + k) % 4))
-    for k in (1, 3):
-        greet(me.at(x=(me.x + k) % 4))
-    for k in (1, 2, 3):
-        greet(me.at(zl=(me.zl // 4) * 4 + (me.zl + k) % 4))
-    greet(me.at(zl=(me.zl + 4) % 8))
+    for k in range(1, 8):
+        greet(me.at(zl=(me.zl + k) % 8))
     greet(partner)
     greet(sibling)
-    for i in range(8):
-        p = 8 * me.c + i
-        greet(me.at(y=p // 4, x=p % 4, c=from_core), jnp.logical_not((p == me.q) & (from_core == me.c)))
 
     @pl.when(on_line)
     def _():
@@ -154,7 +153,17 @@
             p = (me.q + k) % 16
             greet(me.at(y=p // 4, x=p % 4))
 
-    count = 3 + 2 + 4 + 1 + 1 + 8 - jnp.where(swaps_self, 1, 0) + 8 - jnp.where(on_line, 1, 0)
+    @pl.when(jnp.logical_not(on_line))
+    def _():
+        for k in (1, 2, 3):
+            greet(me.at(y=(me.y + k) % 4))
+        for k in (1, 3):
+            greet(me.at(x=(me.x + k) % 4))
+        for i in range(8):
+            p = 8 * me.c + i
+            greet(me.at(y=p // 4, x=p % 4, c=from_core))
+
+    count = 7 + 1 + 1 + 8 + 1 + jnp.where(on_line, -1, 3) + jnp.where(to_core == me.c, 0, 8)
     pl.semaphore_wait(barrier, count)
 
     slot_of = lambda zl: (zl % 2) * 4 + zl // 2
@@ -264,31 +273,64 @@
         def _():
             zbuf[me.zl // 2, rows] = new
 
-        piece = zbuf.at[me.zl // 2, rows]
-        recv = u_r.at[k * 4 + me.zl // 2]
-        sends.start(piece, piece, u_s.at[k * 7], recv, me.at(zl=far), cond=feeds)
-        for i in (1, 2, 3):
-            sends.start(piece, piece, u_s.at[k * 7 + i], recv, me.at(zl=base + (pos + i) % 4), cond=feeds)
+        for v in (0, 2, 4, 6):
+
+            @pl.when(spot == v)
+            def _():
+                for copy in line_copies(k, v, v):
+                    copy.start()
+
         gather_s.begin(k)
 
+    mirror = lambda v: v + me.zh * (7 - 2 * v)
+    spot = mirror(me.zl)
+    row_of = lambda source: source // 2 + me.zh * (3 - 2 * (source // 2))
+
+    def line_copies(k, v, source):
+        piece = zbuf.at[row_of(source), pl.ds(2 * k, 2)]
+        return [
+            pltpu.make_async_remote_copy(
+                src_ref=piece, dst_ref=piece, send_sem=u_s.at[k * 16 + source * 2 + i], recv_sem=u_r.at[k * 4 + source // 2],
+                device_id=me.at(zl=mirror(child)), device_id_type=MESH,
+            )
+            for i, child in enumerate(TREES[source].get(v, ()))
+        ]
+
     def pass_along_z(k):
-        piece = zbuf.at[far // 2, pl.ds(2 * k, 2)]
-        recv = u_r.at[k * 4 + far // 2]
-        pl.when(feeds)(lambda: arrived(piece, recv, sibling))
-        for i in (1, 2, 3):
-            sends.start(piece, piece, u_s.at[k * 7 + 3 + i], recv, me.at(zl=base + (pos + i) % 4), cond=feeds)
+        for v in range(1, 8):
+
+            @pl.when(spot == v)
+            def _():
+                for source in TREES:
+                    if v != source and v in TREES[source]:
+                        arrived(zbuf.at[row_of(source), pl.ds(2 * k, 2)], u_r.at[k * 4 + source // 2], sibling)
+                        for copy in line_copies(k, v, source):
+                            copy.start()
+
+    def sent_along_z():
+        for v in range(8):
+
+            @pl.when(spot == v)
+            def _():
+                for k in range(4):
+                    for source in TREES:
+                        for copy in line_copies(k, v, source):
+                            copy.wait_send()
 
     def swap(k):
         rows = pl.ds(2 * k, 2)
-        for p in range(4):
-            had = feeds & ((me.zl // 2 == p) | (far // 2 == p))
-            pl.when(jnp.logical_not(had))(lambda: arrived(zbuf.at[p, rows], u_r.at[k * 4 + p], sibling))
+        for source in TREES:
+            p = row_of(source)
+            had = False
+            for v in TREES[source]:
+                had = had | (spot == v)
+            pl.when(jnp.logical_not(had))(lambda: arrived(zbuf.at[p, rows], u_r.at[k * 4 + source // 2], sibling))
             for j in (0, 1):
                 px = 2 * me.c + j
                 here = (me.y == p) & (me.x == px)
                 src, dst = zbuf.at[p, rows, :, pl.ds(256 * j, 256)], lbuf.at[rows, me.n]
                 sends.start(
-                    src, dst, t_s.at[k * 8 + p * 2 + j], t_r.at[k], me.at(y=p, x=px), cond=jnp.logical_not(here)
+                    src, dst, t_s.at[k * 8 + source + j], t_r.at[k], me.at(y=p, x=px), cond=jnp.logical_not(here)
                 )
                 pl.when(here)(pltpu.make_async_copy(src, dst, t_r.at[k]).start)
 
@@ -340,6 +382,7 @@
     gather_s.finish((3,))
     from_sibling(3)
     add(3, 1)
+    sent_along_z()
     sends.drain()
 
 
@@ -366,7 +409,7 @@
             pltpu.VMEM((8, 16, 16, 256), bf16),
             dma(32), dma(32), dma(32), dma(32), dma(64), dma(64),
             dma(8), dma(8), dma(8), dma(8), dma(8), dma(8),
-            dma(4), dma(4), dma(5), dma(5), dma(32), dma(4), dma(28), dma(16), dma(4), dma(4), dma(2),
+            dma(4), dma(4), dma(5), dma(5), dma(32), dma(4), dma(64), dma(16), dma(4), dma(4), dma(2),
         ],
         compiler_params=pltpu.CompilerParams(collective_id=0, has_side_effects=True, vmem_limit_bytes=56 << 20),
         cost_estimate=pl.CostEstimate(flops=1 << 31, bytes_accessed=1 << 21, transcendentals=0),

time: 89.7 us -> 89.7 us (level); the launches traced: 88.3 us -> 89.4 us
  Pallas kernels: 85 us -> 86.1 us
    pallas_call x1, Pallas kernels: 85 us -> 86.1 us  [body(): pl.pallas_call(kernel, out_shape=(out, out), in_specs=[hbm] * 4, out_spec...]
where the time goes in v5:
time: 89.7 us; the launch traced here: 89.4 us
  Pallas kernels  86.1 us (96%)
  local copies, waits for them, and re-layouts  2.72 us (3%)
    pallas_call x1, Pallas kernels, body(): pl.pallas_call(kernel, out_shape=(out, out), in_specs=[hbm] * 4, out_spec...  86.1 us
    unnamed x4, local copies, waits for them, and re-layouts  2.72 us

profile of v5, /device:TPU:25, one launch (start us, length us, event | category | flops | bytes accessed | tf_op | source)
XLA Modules:
  0.0 89.4 jit_solution(8761573262697589770)
XLA Ops:
  0.6 86.1 %shard_map.59 = (f32[256,512]{1,0:T(8,128)}, f32[256,512]{1,0:T(8,128)}) custom-call(bf16[128,256]{1,0:T(8,128)(2,1)} %ctx.1, bf16[256,512]{1,0:T(8,128)(2,1)} %w.1, bf16[4,16,512]{2,1,0:T(8,128)(2,1)} %bitcast.2, bf16[4,16,512]{2,1,0:T(8,128)(2,1)} %bitcast.3), custom_call_target="tpu_custom_call" | custom-call | flops 2147483648 | bytes 2097152 | tf_op jit(solution)/shard_map/pallas_call | solution.py:394
  86.7 0.0 copy-start
  86.7 1.9 %copy.8 = f32[256,512]{1,0:T(8,128)} copy(f32[256,512]{1,0:T(8,128)} %get-tuple-element.4) | data formatting | bytes 1048576
  88.6 0.0 copy-done
  88.6 0.8 copy.9
Async XLA Ops:
  86.7 1.9 %copy-start = (f32[256,512]{1,0:T(8,128)S(1)}, f32[256,512]{1,0:T(8,128)}, u32[]{:S(2)}) copy-start(f32[256,512]{1,0:T(8,128)} %get-tuple-element.5) | copy-start | bytes 1572868

commit v6 on v5

--- a/solution.py
+++ b/solution.py
@@ -317,22 +317,24 @@
                         for copy in line_copies(k, v, source):
                             copy.wait_send()
 
-    def swap(k):
+    def swap(k, first):
         rows = pl.ds(2 * k, 2)
         for source in TREES:
             p = row_of(source)
             had = False
             for v in TREES[source]:
                 had = had | (spot == v)
-            pl.when(jnp.logical_not(had))(lambda: arrived(zbuf.at[p, rows], u_r.at[k * 4 + source // 2], sibling))
+            who = had if first else jnp.logical_not(had)
+            if not first:
+                pl.when(who)(lambda: arrived(zbuf.at[p, rows], u_r.at[k * 4 + source // 2], sibling))
             for j in (0, 1):
                 px = 2 * me.c + j
                 here = (me.y == p) & (me.x == px)
                 src, dst = zbuf.at[p, rows, :, pl.ds(256 * j, 256)], lbuf.at[rows, me.n]
                 sends.start(
-                    src, dst, t_s.at[k * 8 + source + j], t_r.at[k], me.at(y=p, x=px), cond=jnp.logical_not(here)
+                    src, dst, t_s.at[k * 8 + source + j], t_r.at[k], me.at(y=p, x=px), cond=who & jnp.logical_not(here)
                 )
-                pl.when(here)(pltpu.make_async_copy(src, dst, t_r.at[k]).start)
+                pl.when(who & here)(pltpu.make_async_copy(src, dst, t_r.at[k]).start)
 
     def to_sibling(k):
         piece = lbuf.at[pl.ds(2 * k, 2)]
@@ -366,8 +368,9 @@
                 gather_s.level(n, (k,))
         if 0 <= slot - 1 < 4:
             pass_along_z(slot - 1)
+            swap(slot - 1, True)
         if 0 <= slot - 2 < 4:
-            swap(slot - 2)
+            swap(slot - 2, False)
         if 0 <= slot - 5 < 4:
             to_sibling(slot - 5)
         if slot == 7:

time: 89.7 us -> 89.2 us (level)
  no operation moved by 1% of the time
where the time goes in v6:
time: 89.2 us; the launch traced here: 89 us
  Pallas kernels  85.7 us (96%)
  local copies, waits for them, and re-layouts  2.72 us (3%)
    pallas_call x1, Pallas kernels, body(): pl.pallas_call(kernel, out_shape=(out, out), in_specs=[hbm] * 4, out_spec...  85.7 us
    unnamed x4, local copies, waits for them, and re-layouts  2.72 us

profile of v6, /device:TPU:25, one launch (start us, length us, event | category | flops | bytes accessed | tf_op | source)
XLA Modules:
  0.0 89.0 jit_solution(17219510125111850928)
XLA Ops:
  0.6 85.7 %shard_map.59 = (f32[256,512]{1,0:T(8,128)}, f32[256,512]{1,0:T(8,128)}) custom-call(bf16[128,256]{1,0:T(8,128)(2,1)} %ctx.1, bf16[256,512]{1,0:T(8,128)(2,1)} %w.1, bf16[4,16,512]{2,1,0:T(8,128)(2,1)} %bitcast.2, bf16[4,16,512]{2,1,0:T(8,128)(2,1)} %bitcast.3), custom_call_target="tpu_custom_call" | custom-call | flops 2147483648 | bytes 2097152 | tf_op jit(solution)/shard_map/pallas_call | solution.py:397
  86.3 0.0 copy-start
  86.3 1.9 %copy.8 = f32[256,512]{1,0:T(8,128)} copy(f32[256,512]{1,0:T(8,128)} %get-tuple-element.4) | data formatting | bytes 1048576
  88.2 0.0 copy-done
  88.2 0.8 copy.9
Async XLA Ops:
  86.3 1.9 %copy-start = (f32[256,512]{1,0:T(8,128)S(1)}, f32[256,512]{1,0:T(8,128)}, u32[]{:S(2)}) copy-start(f32[256,512]{1,0:T(8,128)} %get-tuple-element.5) | copy-start | bytes 1572868
